TPU v7x, 32 devices: a whole 2x2x4 slice. The times are simulated.
32 devices in a mesh: grp: 2 (over y), leaf: 4 (over z), head: 4 (over x, core).
Axes of the slice: x: 2, y: 2, z: 4, core: 2. Of those that a mesh axis runs over, the one named last changes fastest.
Arguments:
- query: bfloat16 [2560, 8192], P(('grp', 'leaf'), 'head'), parts along dimension 0, may hold values from -100 to 100
- key_value: bfloat16 [2560, 2048], P(('grp', 'leaf'), 'head'), parts along dimension 0, may hold values from -4 to 4
- grad_out: bfloat16 [2560, 8192], P(('grp', 'leaf'), 'head'), parts along dimension 0, may hold values from -6 to 6
- lengths: int32 [40], P(('grp', 'leaf')), parts along dimension 0, may hold values from 1 to 64, 960 in all
- ancestors: int32 [40, 4], P(('grp', 'leaf')), parts along dimension 0, may hold values from -1 to 18, as said below
Outputs:
- grad_query: bfloat16 [2560, 8192], P(('grp', 'leaf'), 'head'), parts along dimension 0
- grad_key_value: bfloat16 [2560, 2048], P(('grp', 'leaf'), 'head'), parts along dimension 0
There are 2 independent parts, one for each index of `grp`. A program takes and returns all parts, laid end to end along the dimension named above; each array names one. Nothing has to cross between parts.
Inputs may be any that keep to these rules, and one draw needn't show every extreme that they name: Segment g sits in slot g % 5 of leaf block g // 5. A segment in slot j lists its j ancestors, entry l being the ancestor in slot l (its chain from the root), and -1 in the other entries. `lengths`: the largest is 64 in every draw.
All inputs are finite; a program needn't handle non-finite values. No bound on the sum of `lengths` on one device may be relied on, other than what follows from the above.
Results may differ from a plain program's by a relative error of at most 0.0075.
Values may be sent and summed in bfloat16 or wider, within the bound.
A program may use at most 64 MiB of HBM per device.

v0:
```python
import jax
import jax.numpy as jnp
from jax import lax
from jax.sharding import PartitionSpec as P

HD = 128
SLOT = 64
SEG_DEV = 5


masked_score = -1e30


def from_partner(block, axis, bit):
    count = lax.axis_size(axis)
    route = []
    for low in range(count):
        high = low | 1 << bit
        if high != low and high < count:
            route += [(low, high), (high, low)]
    return lax.ppermute(block, axis, route)


def as_sent(array):

    def short(part):
        return part.astype(jnp.bfloat16) if part.dtype == jnp.float32 else part

    return jax.tree.map(short, array)


def attend(queries, cotangent, key_rows, allowed, inv_root):
    key_part = key_rows[:, :, 0]
    value_part = key_rows[:, :, 1]
    scores = (
        jnp.einsum("qkgd,tkd->kgqt", queries, key_part, preferred_element_type=jnp.float32)
        * inv_root
    )
    scores = jnp.where(allowed, scores, masked_score)
    row_max = jnp.max(scores, -1, keepdims=True)
    exp_scores = jnp.exp(scores - row_max)
    softmax_w = exp_scores / jnp.sum(exp_scores, -1, keepdims=True)
    weights_b = softmax_w.astype(jnp.bfloat16)
    recomputed = jnp.einsum(
        "kgqt,tkd->qkgd", weights_b, value_part, preferred_element_type=jnp.float32
    )
    row_delta = jnp.sum(cotangent.astype(jnp.float32) * recomputed, -1)
    grad_weights = jnp.einsum(
        "qkgd,tkd->kgqt", cotangent, value_part, preferred_element_type=jnp.float32
    )
    grad_scores = (
        softmax_w * (grad_weights - jnp.transpose(row_delta, (1, 2, 0))[..., None])
    ).astype(jnp.bfloat16)
    grad_q = (
        jnp.einsum("kgqt,tkd->qkgd", grad_scores, key_part, preferred_element_type=jnp.float32)
        * inv_root
    )
    grad_k = (
        jnp.einsum("kgqt,qkgd->tkd", grad_scores, queries, preferred_element_type=jnp.float32)
        * inv_root
    )
    grad_v = jnp.einsum("kgqt,qkgd->tkd", weights_b, cotangent, preferred_element_type=jnp.float32)
    grads = jnp.stack([grad_k, grad_v], 2)
    return (grad_q, grads.reshape(grads.shape[0], -1))


def split_halves(merged, head_index, level_bit):
    half_width = merged.shape[1] // 2
    lower_half = merged[:, :half_width]
    upper_half = merged[:, half_width:]
    upper_bit = head_index >> level_bit & 1
    kept_half = jnp.where(upper_bit == 1, upper_half, lower_half)
    sent_half = jnp.where(upper_bit == 1, lower_half, upper_half)
    return (kept_half, sent_half)


def on_device(query, key_value, grad_out, lengths, ancestors):
    col_width = key_value.shape[1]
    pair_width = 2 * HD
    rounds = (pair_width // col_width).bit_length() - 1 if col_width < pair_width else 0
    head_index = lax.axis_index("head")
    far_rows = (SEG_DEV - 1) * SLOT
    joined = key_value
    for level_bit in range(rounds):
        partner = from_partner(joined, "head", level_bit)
        upper_bit = head_index >> level_bit & 1
        joined = jnp.where(
            upper_bit == 1,
            jnp.concatenate([partner, joined], 1),
            jnp.concatenate([joined, partner], 1),
        )
    far_kv, far_lengths = (
        lax.all_gather(joined[:far_rows], "leaf", axis=0, tiled=True),
        lax.all_gather(lengths[: SEG_DEV - 1], "leaf", axis=0, tiled=True),
    )
    local_kv = joined.shape[1] // pair_width
    local_q = query.shape[1] // HD
    group_q = local_q // local_kv
    inv_root = HD ** (-0.5)
    positions = jnp.arange(SLOT)
    far_total = far_kv.shape[0]
    far_pieces = []
    far_starts = []
    own_parts = []
    grad_parts = []
    for slot_index in range(SEG_DEV):
        row_start = slot_index * SLOT
        row_valid = positions < lengths[slot_index]
        queries = query[row_start : row_start + SLOT].reshape(SLOT, local_kv, group_q, HD)
        cotangent = jnp.where(
            row_valid[:, None], grad_out[row_start : row_start + SLOT], jnp.zeros((), jnp.bfloat16)
        )
        cotangent = cotangent.reshape(SLOT, local_kv, group_q, HD)
        pieces = []
        key_masks = []
        slot_starts = []
        for level_index in range(slot_index):
            segment_id = ancestors[slot_index, level_index]
            block_index = segment_id // SEG_DEV * (SEG_DEV - 1) + segment_id % SEG_DEV
            block_start = block_index * SLOT
            pieces.append(lax.dynamic_slice_in_dim(far_kv, block_start, SLOT, 0))
            key_masks.append(
                jnp.broadcast_to(positions[None, :] < far_lengths[block_index], (SLOT, SLOT))
            )
            slot_starts.append(block_start)
        pieces.append(joined[row_start : row_start + SLOT])
        key_masks.append((positions[None, :] <= positions[:, None]) & row_valid[None, :])
        key_rows = jnp.concatenate(pieces, 0).reshape(-1, local_kv, 2, HD)
        grad_q, grad_kv = attend(
            queries, cotangent, key_rows, jnp.concatenate(key_masks, 1), inv_root
        )
        for level_index, block_start in enumerate(slot_starts):
            far_pieces.append(grad_kv[level_index * SLOT : (level_index + 1) * SLOT])
            far_starts.append(block_start)
        own_parts.append(grad_kv[slot_index * SLOT :])
        grad_parts.append(grad_q.reshape(SLOT, local_q * HD))
    far_grad = jnp.zeros((far_total, joined.shape[1]), jnp.float32)
    for piece, block_start in zip(far_pieces, far_starts):
        current = lax.dynamic_slice_in_dim(far_grad, block_start, SLOT, 0)
        far_grad = lax.dynamic_update_slice_in_dim(far_grad, current + piece, block_start, 0)
    merged = jnp.concatenate([far_grad] + own_parts, 0)
    for level_bit in reversed(range(rounds)):
        kept_half, sent_half = split_halves(merged, head_index, level_bit)
        merged = kept_half + from_partner(as_sent(sent_half), "head", level_bit).astype(
            sent_half.dtype
        )
    far_merged = merged[:far_total]
    own_sum = merged[far_total:]
    far_sum = lax.psum_scatter(
        far_merged.astype(jnp.bfloat16), "leaf", scatter_dimension=0, tiled=True
    ).astype(jnp.float32)
    combined = own_sum + jnp.concatenate([far_sum, jnp.zeros((SLOT, col_width), jnp.float32)], 0)
    return (jnp.concatenate(grad_parts, 0).astype(jnp.bfloat16), combined.astype(jnp.bfloat16))


def solution(mesh):
    return jax.shard_map(
        on_device,
        mesh=mesh,
        in_specs=(
            P(("grp", "leaf"), "head"),
            P(("grp", "leaf"), "head"),
            P(("grp", "leaf"), "head"),
            P(("grp", "leaf")),
            P(("grp", "leaf"), None),
        ),
        out_specs=(P(("grp", "leaf"), "head"), P(("grp", "leaf"), "head")),
        check_vma=False,
    )
```

profile of v0, /device:TPU:0, one launch (start us, length us, event | category | flops | bytes accessed | tf_op | source)
XLA Modules:
  0.0 137.1 jit_solution(5325124681015382627)
XLA Ops:
  7.3 1.1 slice.216
  8.3 0.8 copy.126
  9.3 1.7 %fusion.143 = (s32[1,1]{0,1:T(1,128)}, s32[1,1]{0,1:T(1,128)}, s32[1,1]{0,1:T(1,128)}, s32[1,1]{0,1:T(1,128)}, s32[1,1]{0,1:T(1,128)}, /*index=5*/s32[1,1]{0,1:T...) fusion(s32[5,4]{0,1:T(4,128)} %param.9), kind=kLoop, calls=%fused_computation.264 | loop fusion | bytes 80 | tf_op jit(solution)/shard_map/slice | solution.py:118
  29.8 0.7 fusion.144
  30.4 0.6 dynamic-slice
  31.8 9.9 %all-reduce.1 = s32[16]{0:T(128)S(1)} all-reduce(s32[16]{0:T(128)S(1)} %slice_dynamic-update-slice_fusion), channel_id=1, replica_groups=mesh['grp'=2,'leaf'=4,'head'=4] {'leaf'}, use_global_device_ids=true, to_apply=%add.1 | all-reduce | flops 16 | bytes 128
  41.7 0.6 iota_compare_fusion.15
  42.4 0.7 fusion.145
  43.1 0.6 iota_compare_fusion.2
  43.7 0.6 iota_compare_fusion.3
  44.4 0.6 iota_compare_fusion.4
  44.9 0.6 iota_compare_fusion.5
  45.5 0.6 iota_compare_fusion.9
  46.1 0.6 iota_compare_fusion.14
  46.8 1.3 iota_compare_fusion.10
  48.2 0.7 fusion.111
  48.9 1.3 iota_compare_fusion.1
  50.2 0.7 constant_dynamic-update-slice_fusion.4
  50.9 0.7 fusion.142
  51.7 0.7 constant_dynamic-update-slice_fusion.3
  52.3 0.7 constant_dynamic-update-slice_fusion.2
  53.0 0.7 constant_dynamic-update-slice_fusion.1
  53.7 0.7 constant_dynamic-update-slice_fusion
  54.6 1.1 copy-done.1
  55.8 0.8 copy.139
  56.6 1.2 iota_compare_fusion.7
  57.8 1.3 iota_compare_fusion.11
  59.5 1.4 %fusion.146 = (f32[2,8,64]{2,1,0:T(8,128)S(1)}, f32[2,8,64,64]{2,3,1,0:T(8,128)S(1)}) fusion(pred[64,64]{0,1:T(8,128)(4,1)} %fusion.111, bf16[64,2,8,128]{3,2,1,0:T(8,128)(2,1)} %bitcast.501, bf16[64,2,1,128]{3,2,1,0:T(2,128)(2,1)S(1)} %get-tuple-element.42), kind=kOutput, calls=%fused_computation.267 | convolution fusion | flops 17039424 | bytes 565248 | tf_op jit(solution)/shard_map/sub | solution.py:41
  61.0 1.9 %fusion.49 = f32[64,2,8]{0,2,1:T(8,128)} fusion(bf16[2,8,64,64]{2,3,1,0:T(8,128)(2,1)S(1)} %fusion.89, bf16[64,2,8,128]{3,2,1,0:T(8,128)(2,1)S(1)} %bitcast.461, bf16[64,2,1,128]{3,2,1,0:T(2,128)(2,1)} %get-tuple-element.41), kind=kOutput, calls=%fused_computation.71 | convolution fusion | flops 17169408 | bytes 430080 | tf_op jit(solution)/shard_map/kgqt,tkd->qkgd/dot_general | solution.py:44
  63.2 0.7 copy.28
  63.9 0.7 copy.37
  64.7 1.5 %copy.54 = pred[64,320]{1,0:T(8,128)(4,1)} copy(pred[64,320]{0,1:T(8,128)(4,1)} %constant_dynamic-update-slice_fusion) | data formatting | bytes 40960 | tf_op jit(solution)/shard_map/concatenate | solution.py:130
  66.2 0.8 copy.136
  66.9 0.7 copy.133
  67.8 0.8 copy.127
  68.8 0.7 copy.151
  69.5 0.7 copy.145
  70.3 0.8 copy.148
  72.8 0.7 constant_dynamic-update-slice_fusion.9
  73.5 0.8 bitcast_dynamic-update-slice_fusion.4
  74.3 2.6 %constant_dynamic-slice_fusion = (bf16[64,512]{0,1:T(8,128)(2,1)}, bf16[64,512]{0,1:T(8,128)(2,1)}, bf16[64,512]{0,1:T(8,128)(2,1)}, bf16[64,512]{0,1:T(8,128)(2...) fusion(bf16[1024,512]{0,1:T(8,128)(2,1)} %all-gather.2.cloned.1, ...), kind=kLoop, calls=%fused_computation.219 | loop fusion | bytes 1310760 | tf_op jit(solution)/shard_map/dynamic_slice | solution.py:121
  77.0 0.5 fusion.149
  78.1 1.0 convolution_bitcast_fusion.15
  79.5 0.9 fusion.64
  80.8 0.5 fusion.155
  82.0 1.2 convolution_bitcast_fusion.11
  83.6 1.1 fusion.57
  85.1 0.6 fusion.152
  86.3 0.5 convolution_bitcast_fusion.13
  87.1 0.6 copy-done.17
  87.8 1.0 fusion.62
  89.4 1.9 %fusion.158 = (f32[2,8,64]{2,1,0:T(8,128)S(1)}, f32[2,8,64,320]{3,2,1,0:T(8,128)S(1)}) fusion(pred[64,320]{1,0:T(8,128)(4,1)S(1)} %copy-done.25, bf16[64,2,8,128]{3,2,1,0:T(8,128)(2,1)} %bitcast.497, bf16[320,2,2,128]{0,3,2,1:T(8,128)(2,1)S(1)} %bitcast.481), kind=kOutput, calls=%fused_computation.271 | convolution fusion | flops 85197120 | bytes 1798144 | tf_op jit(solution)/shard_map/sub | solution.py:41
  91.4 0.5 fusion.53
  91.9 0.6 convolution_bitcast_fusion.9
  93.5 1.2 fusion.48
  95.9 0.9 pad_maximum_fusion.4
  97.5 1.0 pad_maximum_fusion.2
  100.1 1.1 convert_element_type.68
  102.5 0.8 bitcast_dynamic-update-slice_fusion.3
  103.2 0.8 bitcast_dynamic-update-slice_fusion.2
  104.0 0.8 bitcast_dynamic-update-slice_fusion.1
  104.7 0.8 bitcast_dynamic-update-slice_fusion
  105.5 23.0 %reduce-scatter.2.cloned.1.call-done = bf16[256,512]{1,0:T(8,128)(2,1)} async-done(((bf16[1024,512]{1,0:T(8,128)(2,1)}), bf16[256,512]{1,0:T(8,128)(2,1)}) %reduce-scatter.2.cloned.1.call-update) | async-done | bytes 262160 | tf_op jit(solution)/shard_map/reduce_scatter | solution.py:149
  128.5 1.8 %add_convert_fusion = bf16[320,512]{1,0:T(8,128)(2,1)} fusion(f32[320,512]{1,0:T(8,128)S(1)} %constant_dynamic-update-slice_fusion.5, bf16[256,512]{1,0:T(8,128)(2,1)} %reduce-scatter.2.cloned.1.call-done), kind=kLoop, calls=%fused_computation.113 | loop fusion | flops 491520 | bytes 1245184 | tf_op jit(solution)/shard_map/convert_element_type | solution.py:153
  (170 shorter events, 13.5 us)
Async XLA Ops:
  7.2 23.3 %copy-start.31 = (u32[32]{0:T(128)S(1)}, u32[32]{0:T(128)}, u32[]{:S(2)}) copy-start(u32[32]{0:T(128)} %constant.132) | copy-start | bytes 388
  7.2 22.6 %copy-start.2 = (bf16[320,512]{1,0:T(8,128)(2,1)S(1)}, bf16[320,512]{1,0:T(8,128)(2,1)}, u32[]{:S(2)}) copy-start(bf16[320,512]{1,0:T(8,128)(2,1)} %param.6) | copy-start | bytes 983044
  7.2 22.6 %copy-start.27 = (s32[5]{0:T(128)S(1)}, s32[5]{0:T(128)}, u32[]{:S(2)}) copy-start(s32[5]{0:T(128)} %param.8) | copy-start | bytes 64
  7.2 47.2 %copy-start = (bf16[320,2048]{1,0:T(8,128)(2,1)S(1)}, bf16[320,2048]{1,0:T(8,128)(2,1)}, u32[]{:S(2)}) copy-start(bf16[320,2048]{1,0:T(8,128)(2,1)} %param.7) | copy-start | bytes 3932164
  7.2 67.0 %all-gather.2.cloned.1.call-start = ((), (), s32[]{:S(2)}) async-start(), calls=%async_computation.1 | async-start | bytes 1310720 | tf_op jit(solution)/shard_map/all_gather | solution.py:93
  9.2 119.3 %reduce-scatter.2.cloned.1.call-start = ((), (), s32[]{:S(2)}) async-start(), calls=%async_computation.2 | async-start | bytes 1310720 | tf_op jit(solution)/shard_map/reduce_scatter | solution.py:149
  51.7 7.9 %copy-start.21 = (bf16[64,2,1,128]{3,2,1,0:T(2,128)(2,1)}, bf16[64,2,1,128]{3,2,1,0:T(2,128)(2,1)S(1)}, u32[]{:S(2)}) copy-start(bf16[64,2,1,128]{3,2,1,0:T(2,128)(2,1)S(1)} %get-tuple-element.42) | copy-start | bytes 98308
  54.4 1.3 copy-start.1
  60.9 2.0 %copy-start.6 = (f32[2,8,64,64]{2,3,1,0:T(8,128)}, f32[2,8,64,64]{2,3,1,0:T(8,128)S(1)}, u32[]{:S(2)}) copy-start(f32[2,8,64,64]{2,3,1,0:T(8,128)S(1)} %get-tuple-element.69) | copy-start | bytes 786436
  60.9 3.0 %copy-start.28 = (f32[2,8,64]{2,1,0:T(8,128)}, f32[2,8,64]{2,1,0:T(8,128)S(1)}, u32[]{:S(2)}) copy-start(f32[2,8,64]{2,1,0:T(8,128)S(1)} %get-tuple-element.68) | copy-start | bytes 12292
  68.7 2.4 %copy-start.7 = (f32[2,8,64,64]{2,3,1,0:T(8,128)S(1)}, f32[2,8,64,64]{2,3,1,0:T(8,128)}, u32[]{:S(2)}) copy-start(f32[2,8,64,64]{2,3,1,0:T(8,128)} %copy-done.6) | copy-start | bytes 786436
  68.7 2.4 %copy-start.24 = (bf16[64,2,1,128]{3,2,1,0:T(2,128)(2,1)S(1)}, bf16[64,2,1,128]{3,2,1,0:T(2,128)(2,1)}, u32[]{:S(2)}) copy-start(bf16[64,2,1,128]{3,2,1,0:T(2,128)(2,1)} %get-tuple-element.41) | copy-start | bytes 98308
  68.7 2.4 %copy-start.29 = (f32[2,8,64]{2,1,0:T(8,128)S(1)}, f32[2,8,64]{2,1,0:T(8,128)}, u32[]{:S(2)}) copy-start(f32[2,8,64]{2,1,0:T(8,128)} %copy-done.28) | copy-start | bytes 12292
  68.7 2.4 %copy-start.32 = (f32[64,2,8]{0,2,1:T(8,128)S(1)}, f32[64,2,8]{0,2,1:T(8,128)}, u32[]{:S(2)}) copy-start(f32[64,2,8]{0,2,1:T(8,128)} %fusion.49) | copy-start | bytes 12292
  70.3 1.2 copy-start.22
  71.1 1.0 copy-start.18
  73.5 3.4 %copy-start.5 = (bf16[64,512]{0,1:T(8,128)(2,1)S(1)}, bf16[64,512]{0,1:T(8,128)(2,1)}, u32[]{:S(2)}) copy-start(bf16[64,512]{0,1:T(8,128)(2,1)} %copy.127) | copy-start | bytes 196612
  74.2 2.7 %copy-start.30 = (pred[64,128]{1,0:T(8,128)(4,1)S(1)}, pred[64,128]{1,0:T(8,128)(4,1)}, u32[]{:S(2)}) copy-start(pred[64,128]{1,0:T(8,128)(4,1)} %copy.28) | copy-start | bytes 24580
  79.1 1.5 %copy-start.9 = (bf16[64,512]{0,1:T(8,128)(2,1)S(1)}, bf16[64,512]{0,1:T(8,128)(2,1)}, u32[]{:S(2)}) copy-start(bf16[64,512]{0,1:T(8,128)(2,1)} %copy.133) | copy-start | bytes 196612
  79.4 1.4 %copy-start.19 = (bf16[8,8,16,128]{3,2,1,0:T(8,128)(2,1)S(1)}, bf16[8,8,16,128]{3,2,1,0:T(8,128)(2,1)}, u32[]{:S(2)}) copy-start(bf16[8,8,16,128]{3,2,1,0:T(8,128)(2,1)} %copy.148) | copy-start | bytes 786436
  83.6 1.5 %copy-start.16 = (bf16[8,8,16,128]{3,2,1,0:T(8,128)(2,1)S(1)}, bf16[8,8,16,128]{3,2,1,0:T(8,128)(2,1)}, u32[]{:S(2)}) copy-start(bf16[8,8,16,128]{3,2,1,0:T(8,128)(2,1)} %copy.145) | copy-start | bytes 786436
  83.6 1.5 %copy-start.26 = (pred[64,192]{1,0:T(8,128)(4,1)S(1)}, pred[64,192]{1,0:T(8,128)(4,1)}, u32[]{:S(2)}) copy-start(pred[64,192]{1,0:T(8,128)(4,1)} %copy.37) | copy-start | bytes 36868
  86.8 1.0 copy-start.17
  87.7 1.3 copy-start.10
  87.7 1.3 copy-start.11
  87.7 1.4 copy-start.12
  87.7 1.4 copy-start.13
  87.7 1.4 copy-start.14
  87.7 1.6 %copy-start.25 = (pred[64,320]{1,0:T(8,128)(4,1)S(1)}, pred[64,320]{1,0:T(8,128)(4,1)}, u32[]{:S(2)}) copy-start(pred[64,320]{1,0:T(8,128)(4,1)} %copy.54) | copy-start | bytes 61444
  92.5 1.0 copy-start.15
  92.9 1.7 %copy-start.8 = (f32[128,2,1,128]{3,0,1,2:T(8,128)S(1)}, f32[128,2,1,128]{3,0,1,2:T(8,128)}, u32[]{:S(2)}) copy-start(f32[128,2,1,128]{3,0,1,2:T(8,128)} %convolution_bitcast_fusion.15) | copy-start | bytes 393220
  93.0 1.7 %copy-start.23 = (f32[128,2,1,128]{3,0,1,2:T(8,128)S(1)}, f32[128,2,1,128]{3,0,1,2:T(8,128)}, u32[]{:S(2)}) copy-start(f32[128,2,1,128]{3,0,1,2:T(8,128)} %fusion.64) | copy-start | bytes 393220
  93.5 1.6 %copy-start.3 = (f32[256,2,1,128]{3,0,1,2:T(8,128)S(1)}, f32[256,2,1,128]{3,0,1,2:T(8,128)}, u32[]{:S(2)}) copy-start(f32[256,2,1,128]{3,0,1,2:T(8,128)} %convolution_bitcast_fusion.11) | copy-start | bytes 786436
  93.5 1.6 %copy-start.20 = (f32[256,2,1,128]{3,0,1,2:T(8,128)S(1)}, f32[256,2,1,128]{3,0,1,2:T(8,128)}, u32[]{:S(2)}) copy-start(f32[256,2,1,128]{3,0,1,2:T(8,128)} %fusion.57) | copy-start | bytes 786436
  100.0 1.2 copy-start.4
Sparse Core Ops, SparseCore 0:
  9.6 32.8 all-gather.1
  101.3 27.1 reduce-scatter.1
where the time goes:
time: 138 us; the launch traced here: 137 us
  between operations  34.7 us (25%)
  local copies, waits for them, and re-layouts  31.9 us (23%)
  waiting for transfers between devices  23.1 us (17%)
  matrix products  19.6 us (14%)
  other arithmetic  18 us (13%)
  blocking collectives  9.9 us (7%)
    reduce_scatter x1, waiting for transfers between devices, on_device(): lax.psum_scatter(far_merged.astype(jnp.bfloat16), 'leaf', scatter_dimensi...  23 us
    unnamed x97, local copies, waits for them, and re-layouts  15.8 us
    unnamed x1, blocking collectives  9.9 us
    lt x8, other arithmetic, on_device(): positions[None, :] < far_lengths[block_index]  6.13 us
    sub x5, matrix products, attend(): exp_scores = jnp.exp(scores - row_max)  4.82 us
    dot_general x5, matrix products, attend(): jnp.einsum('kgqt,qkgd->tkd', grad_scores, queries, preferred_element_type...  4.38 us
    dot_general x5, matrix products, attend(): jnp.einsum('kgqt,qkgd->tkd', weights_b, cotangent, preferred_element_type...  3.57 us
    dot_general x5, matrix products, attend(): jnp.einsum('kgqt,tkd->qkgd', weights_b, value_part, preferred_element_typ...  3.52 us
  transfers between devices with their start and end apart: 2, of which 1 were waited for; matrix products, arithmetic and copies ran while one was open for 28% of the time, Pallas kernels for 0%

commit v1 on v0

--- a/solution.py
+++ b/solution.py
@@ -1,6 +1,11 @@
+import functools
+import math
+
 import jax
 import jax.numpy as jnp
 from jax import lax
+from jax.experimental import pallas as pl
+from jax.experimental.pallas import tpu as pltpu
 from jax.sharding import PartitionSpec as P
 
 HD = 128
@@ -74,7 +79,7 @@
     return (kept_half, sent_half)
 
 
-def on_device(query, key_value, grad_out, lengths, ancestors):
+def general_device(query, key_value, grad_out, lengths, ancestors):
     col_width = key_value.shape[1]
     pair_width = 2 * HD
     rounds = (pair_width // col_width).bit_length() - 1 if col_width < pair_width else 0
@@ -153,6 +158,340 @@
     return (jnp.concatenate(grad_parts, 0).astype(jnp.bfloat16), combined.astype(jnp.bfloat16))
 
 
+FAR = SEG_DEV - 1
+PAIRS = [(slot, level) for slot in range(SEG_DEV) for level in range(slot)]
+F32 = jnp.float32
+BF16 = jnp.bfloat16
+
+
+def dot(left, right, left_dim, right_dim):
+    return lax.dot_general(
+        left, right, (((left_dim,), (right_dim,)), ((), ())), preferred_element_type=F32
+    )
+
+
+def kernel(n, kvh, group, lengths, ancestors, query, key_value, grad_out, dq_out, dkv_out, *scratch):
+    scratch = list(scratch)
+    kv_buf = [[scratch.pop(0) for _ in range(FAR)] for _ in range(kvh)]
+    last_kv, q_buf, do_buf, dq_buf, dkv_buf, lens, own, term, sent, arrived = scratch[:10]
+    kv_in, last_in, q_in, do_in, dq_sem, dkv_sem, kv_send, kv_recv, len_send, len_recv, g_send, g_recv = scratch[10:]
+    me = lax.axis_index("leaf")
+    inv_root = HD ** (-0.5)
+    width = 2 * HD
+    cols = group * HD
+
+    def kv_local(h, l):
+        return pltpu.make_async_copy(
+            key_value.at[pl.ds(l * SLOT, SLOT), pl.ds(h * width, width)], kv_buf[h][l].at[me], kv_in.at[h, l]
+        )
+
+    def last_local(h):
+        return pltpu.make_async_copy(
+            key_value.at[pl.ds(FAR * SLOT, SLOT), pl.ds(h * width, width)], last_kv.at[h], last_in.at[h]
+        )
+
+    def rows_in(source, target, sem, j):
+        rows = pl.ds(j * SLOT, SLOT)
+        return pltpu.make_async_copy(source.at[rows], target.at[rows], sem.at[j])
+
+    for h in range(kvh):
+        for l in range(FAR):
+            kv_local(h, l).start()
+    for h in range(kvh):
+        last_local(h).start()
+    for j in range(SEG_DEV):
+        rows_in(query, q_buf, q_in, j).start()
+        rows_in(grad_out, do_buf, do_in, j).start()
+
+    barrier = pltpu.get_barrier_semaphore()
+    for k in range(1, n):
+        pl.semaphore_signal(
+            barrier, inc=1, device_id={"leaf": lax.rem(me + k, n)}, device_id_type=pl.DeviceIdType.MESH
+        )
+    for l in range(FAR):
+        lens[me, l] = jnp.full((128,), lengths[l], jnp.int32)
+    pl.semaphore_wait(barrier, n - 1)
+
+    def lens_copy(k):
+        return pltpu.make_async_remote_copy(
+            src_ref=lens.at[me],
+            dst_ref=lens.at[me],
+            send_sem=len_send.at[k - 1],
+            recv_sem=len_recv.at[k - 1],
+            device_id={"leaf": lax.rem(me + k, n)},
+            device_id_type=pl.DeviceIdType.MESH,
+        )
+
+    def hop_ok(way, s):
+        if way == 0:
+            return (me < n - 1) & (me - s >= 0)
+        return (me > 0) & (me + s <= n - 1)
+
+    def got_ok(way, s):
+        return me - 1 - s >= 0 if way == 0 else me + 1 + s <= n - 1
+
+    def kv_copy(way, s, h, l, block):
+        ref = kv_buf[h][l].at[block]
+        return pltpu.make_async_remote_copy(
+            src_ref=ref,
+            dst_ref=ref,
+            send_sem=kv_send.at[way, s, h, l],
+            recv_sem=kv_recv.at[way, s, h, l],
+            device_id={"leaf": me + 1 if way == 0 else me - 1},
+            device_id_type=pl.DeviceIdType.MESH,
+        )
+
+    def kv_start(way, s, h, l):
+        @pl.when(hop_ok(way, s))
+        def _():
+            kv_copy(way, s, h, l, me - s if way == 0 else me + s).start()
+
+    def kv_arrive(way, s, h, l):
+        @pl.when(got_ok(way, s))
+        def _():
+            kv_copy(way, s, h, l, me - 1 - s if way == 0 else me + 1 + s).wait_recv()
+
+    def own_sends(h):
+        for l in range(FAR):
+            kv_start(0, 0, h, l)
+            kv_start(1, 0, h, l)
+
+    def hop(h, s):
+        for l in range(FAR):
+            for way in (0, 1):
+                kv_arrive(way, s, h, l)
+                if s + 1 < n - 1:
+                    kv_start(way, s + 1, h, l)
+
+    key_pos = lax.broadcasted_iota(jnp.int32, (SLOT, 128), 0)
+    query_pos = lax.broadcasted_iota(jnp.int32, (SLOT, 128), 1) & (SLOT - 1)
+    parts = 2 if group % 4 == 0 else 1
+    heads = group // parts
+    lanes = heads * SLOT
+
+    def wide(tile):
+        return jnp.concatenate([tile] * (lanes // 128), 1)
+
+    def home(j, l):
+        return lax.div(ancestors[j, l], SEG_DEV)
+
+    def dq_copy(h, j):
+        view = (pl.ds(j * SLOT, SLOT), pl.ds(h * cols, cols))
+        return pltpu.make_async_copy(dq_buf.at[view], dq_out.at[view], dq_sem.at[h, j])
+
+    def compute(h, j):
+        rows = pl.ds(j * SLOT, SLOT)
+        pieces, biases = [], []
+        for l in range(j):
+            place = home(j, l)
+            pieces.append(kv_buf[h][l][place])
+            biases.append(jnp.where(key_pos < lens[place, l : l + 1, :], 0.0, masked_score))
+        pieces.append(kv_buf[h][j][me] if j < FAR else last_kv[h])
+        biases.append(
+            jnp.where((key_pos < lengths[j]) & (key_pos <= query_pos), 0.0, masked_score)
+        )
+        keys = jnp.concatenate([piece[:, :HD] for piece in pieces], 0)
+        values = jnp.concatenate([piece[:, HD:] for piece in pieces], 0)
+        bias = wide(jnp.concatenate(biases, 0))
+        valid = jnp.where(key_pos < lengths[j], 1.0, 0.0).astype(BF16)
+        grad_k = grad_v = None
+        for part in range(parts):
+            at = [(h * group + part * heads + g) * HD for g in range(heads)]
+            q = jnp.concatenate([q_buf[rows, pl.ds(a, HD)] for a in at], 0)
+            do = jnp.concatenate([do_buf[rows, pl.ds(a, HD)] * valid for a in at], 0)
+            scores = dot(keys, q, 1, 1) * (inv_root * math.log2(math.e)) + bias
+            top = jnp.max(scores, 0, keepdims=True)
+            powers = jnp.exp2(scores - top)
+            probs = powers * (1.0 / jnp.sum(powers, 0, keepdims=True))
+            probs_b = probs.astype(BF16)
+            dprobs = dot(values, do, 1, 1)
+            delta = jnp.sum(probs_b.astype(F32) * dprobs, 0, keepdims=True)
+            dscores = (probs * (dprobs - delta)).astype(BF16)
+            part_v = dot(probs_b, do, 1, 0)
+            part_k = dot(dscores, q, 1, 0)
+            grad_v = part_v if grad_v is None else grad_v + part_v
+            grad_k = part_k if grad_k is None else grad_k + part_k
+            grad_q = (dot(dscores, keys, 0, 0) * inv_root).astype(BF16)
+            for g, a in enumerate(at):
+                dq_buf[rows, pl.ds(a, HD)] = grad_q[g * SLOT : (g + 1) * SLOT]
+        dq_copy(h, j).start()
+        grads = jnp.concatenate([grad_k * inv_root, grad_v], 1)
+        for l in range(j):
+            term[h, PAIRS.index((j, l))] = grads[l * SLOT : (l + 1) * SLOT]
+        own[h, j] = grads[j * SLOT :]
+
+    def local_terms(h, l, target):
+        total = None
+        for j in range(l + 1, SEG_DEV):
+            weight = jnp.where(home(j, l) == target, 1.0, 0.0).astype(F32)
+            one = term[h, PAIRS.index((j, l))] * weight
+            total = one if total is None else total + one
+        return total
+
+    def g_copy(way, k, h, l, target):
+        return pltpu.make_async_remote_copy(
+            src_ref=sent.at[h, target, l],
+            dst_ref=arrived.at[way, h, target, l],
+            send_sem=g_send.at[way, k - 1, h, l],
+            recv_sem=g_recv.at[way, k - 1, h, l],
+            device_id={"leaf": me + 1 if way == 0 else me - 1},
+            device_id_type=pl.DeviceIdType.MESH,
+        )
+
+    def g_target(way, k):
+        return me + k if way == 0 else me - k
+
+    def g_ok(way, k):
+        return me + k <= n - 1 if way == 0 else me - k >= 0
+
+    def g_behind(way):
+        return me > 0 if way == 0 else me < n - 1
+
+    def send_terms(h, k):
+        for l in range(FAR):
+            for way in (0, 1):
+                @pl.when(g_ok(way, k))
+                def _():
+                    target = g_target(way, k)
+                    sent[h, target, l] = local_terms(h, l, target).astype(BF16)
+
+                    if k < n - 1:
+                        @pl.when(g_behind(way))
+                        def _():
+                            g_copy(way, k + 1, h, l, target).wait_recv()
+                            total = sent[h, target, l].astype(F32) + arrived[way, h, target, l].astype(F32)
+                            sent[h, target, l] = total.astype(BF16)
+
+                    g_copy(way, k, h, l, target).start()
+
+    def dkv_copy(h, j):
+        view = (pl.ds(j * SLOT, SLOT), pl.ds(h * width, width))
+        return pltpu.make_async_copy(dkv_buf.at[view], dkv_out.at[view], dkv_sem.at[h, j])
+
+    def finish_last(h):
+        dkv_buf[pl.ds(FAR * SLOT, SLOT), pl.ds(h * width, width)] = own[h, FAR].astype(BF16)
+        dkv_copy(h, FAR).start()
+
+    def finish(h):
+        for l in range(FAR):
+            own[h, l] = own[h, l] + local_terms(h, l, me).astype(BF16).astype(F32)
+            for way in (0, 1):
+                @pl.when(g_behind(way))
+                def _():
+                    g_copy(way, 1, h, l, me).wait_recv()
+                    own[h, l] = own[h, l] + arrived[way, h, me, l].astype(F32)
+            dkv_buf[pl.ds(l * SLOT, SLOT), pl.ds(h * width, width)] = own[h, l].astype(BF16)
+            dkv_copy(h, l).start()
+
+    for k in range(1, n):
+        lens_copy(k).start()
+    for l in range(FAR):
+        kv_local(0, l).wait()
+        kv_start(0, 0, 0, l)
+        kv_start(1, 0, 0, l)
+    for h in range(1, kvh):
+        for l in range(FAR):
+            kv_local(h, l).wait()
+    for h in range(kvh):
+        last_local(h).wait()
+    for k in range(1, n):
+        lens_copy(k).wait()
+    for j in range(SEG_DEV):
+        rows_in(query, q_buf, q_in, j).wait()
+        rows_in(grad_out, do_buf, do_in, j).wait()
+
+    for h in range(kvh):
+        compute(h, 0)
+    for s in range(n - 1):
+        hop(0, s)
+    for h in range(kvh):
+        steps = []
+        if h + 1 < kvh:
+            own_sends(h + 1)
+            steps += [functools.partial(hop, h + 1, s) for s in range(n - 1)]
+        if h > 0:
+            steps += [functools.partial(send_terms, h - 1, k) for k in range(n - 1, 0, -1)]
+        for j in range(1, SEG_DEV):
+            if steps and h > 0:
+                steps.pop(0)()
+            compute(h, j)
+            if steps and h == 0:
+                steps.pop(0)()
+        for step in steps:
+            step()
+        finish_last(h)
+    for k in range(n - 1, 0, -1):
+        send_terms(kvh - 1, k)
+    for h in range(kvh):
+        finish(h)
+
+    for k in range(1, n):
+        for way in (0, 1):
+            @pl.when(g_ok(way, k))
+            def _():
+                for h in range(kvh):
+                    for l in range(FAR):
+                        g_copy(way, k, h, l, g_target(way, k)).wait_send()
+    for s in range(n - 1):
+        for way in (0, 1):
+            @pl.when(hop_ok(way, s))
+            def _():
+                for h in range(kvh):
+                    for l in range(FAR):
+                        kv_copy(way, s, h, l, me - s if way == 0 else me + s).wait_send()
+    for h in range(kvh):
+        for j in range(SEG_DEV):
+            dq_copy(h, j).wait()
+            dkv_copy(h, j).wait()
+
+
+def line_device(query, key_value, grad_out, lengths, ancestors):
+    n = lax.axis_size("leaf")
+    width = 2 * HD
+    kvh = key_value.shape[1] // width
+    group = query.shape[1] // (kvh * HD)
+    tile = (SLOT, width)
+    scratch = [pltpu.VMEM((n,) + tile, BF16) for _ in range(kvh * FAR)]
+    scratch += [
+        pltpu.VMEM((kvh,) + tile, BF16),
+        pltpu.VMEM(query.shape, BF16),
+        pltpu.VMEM(query.shape, BF16),
+        pltpu.VMEM(query.shape, BF16),
+        pltpu.VMEM(key_value.shape, BF16),
+        pltpu.VMEM((n, 8, 128), jnp.int32),
+        pltpu.VMEM((kvh, SEG_DEV) + tile, F32),
+        pltpu.VMEM((kvh, len(PAIRS)) + tile, F32),
+        pltpu.VMEM((kvh, n, FAR) + tile, BF16),
+        pltpu.VMEM((2, kvh, n, FAR) + tile, BF16),
+    ]
+    dma = pltpu.SemaphoreType.DMA
+    scratch += [dma((kvh, FAR)), dma((kvh,)), dma((SEG_DEV,)), dma((SEG_DEV,))]
+    scratch += [dma((kvh, SEG_DEV)), dma((kvh, SEG_DEV))]
+    scratch += [dma((2, n - 1, kvh, FAR)), dma((2, n - 1, kvh, FAR)), dma((n - 1,)), dma((n - 1,))]
+    scratch += [dma((2, n - 1, kvh, FAR)), dma((2, n - 1, kvh, FAR))]
+    smem = pl.BlockSpec(memory_space=pltpu.SMEM)
+    anywhere = pl.BlockSpec(memory_space=pl.ANY)
+    return pl.pallas_call(
+        functools.partial(kernel, n, kvh, group),
+        out_shape=(
+            jax.ShapeDtypeStruct(query.shape, BF16),
+            jax.ShapeDtypeStruct(key_value.shape, BF16),
+        ),
+        in_specs=[smem, smem, anywhere, anywhere, anywhere],
+        out_specs=(anywhere, anywhere),
+        scratch_shapes=scratch,
+        compiler_params=pltpu.CompilerParams(
+            collective_id=0, has_side_effects=True, vmem_limit_bytes=48 * 1024 * 1024
+        ),
+    )(lengths, ancestors, query, key_value, grad_out)
+
+
+def on_device(query, key_value, grad_out, lengths, ancestors):
+    whole_heads = key_value.shape[1] % (2 * HD) == 0
+    step = line_device if whole_heads else general_device
+    return step(query, key_value, grad_out, lengths, ancestors)
+
+
 def solution(mesh):
     return jax.shard_map(
         on_device,

time: 138 us -> 57.7 us (0.42)
  Pallas kernels: 0 us -> 50 us
  between operations: 34.7 us -> 0.64 us
  local copies, waits for them, and re-layouts: 31.9 us -> 6.81 us
  waiting for transfers between devices: 23.1 us -> 0 us
  matrix products: 19.6 us -> 0 us
  other arithmetic: 18 us -> 0 us
  blocking collectives: 9.9 us -> 0 us
    pallas_call x0 -> x1, Pallas kernels: none -> 50 us  [line_device(): pl.pallas_call(functools.partial(kernel, n, kvh, group), out_shape=(jax.S...]
    reduce_scatter x1 -> x0, waiting for transfers between devices: 23 us -> none  [on_device(): lax.psum_scatter(far_merged.astype(jnp.bfloat16), 'leaf', scatter_dimensi...]
    dot_general x25 -> x0, matrix products: 14.8 us -> none  [the longest x5 4.38 us: attend(): jnp.einsum('kgqt,qkgd->tkd', grad_scores, queries, preferred_element_type...]
    unnamed x1 -> x0, blocking collectives: 9.9 us -> none
    lt x11 -> x0, other arithmetic: 9.29 us -> none  [the longest x8 6.13 us: on_device(): positions[None, :] < far_lengths[block_index]]
    unnamed x97 -> x11, local copies, waits for them, and re-layouts: 15.8 us -> 6.81 us
    slice x33 -> x0, local copies, waits for them, and re-layouts: 7.14 us -> none  [the longest x20 2.1 us: on_device(): far_pieces.append(grad_kv[level_index * SLOT:(level_index + 1) * SLOT])]
    sub x5 -> x0, matrix products: 4.82 us -> none  [attend(): exp_scores = jnp.exp(scores - row_max)]
  transfers between devices with their start and end apart: 2 -> 0, of which waited for: 1 -> 0; matrix products, arithmetic and copies ran while one was open for 28% -> 0% of each run, Pallas kernels for 0% -> 0%
where the time goes in v1:
time: 57.7 us; the launch traced here: 57.4 us
  Pallas kernels  50 us (87%)
  local copies, waits for them, and re-layouts  6.81 us (12%)
  between operations  0.64 us (1%)
    pallas_call x1, Pallas kernels, line_device(): pl.pallas_call(functools.partial(kernel, n, kvh, group), out_shape=(jax.S...  50 us
    unnamed x11, local copies, waits for them, and re-layouts  6.81 us

profile of v1, /device:TPU:0, one launch (start us, length us, event | category | flops | bytes accessed | tf_op | source)
XLA Modules:
  0.0 57.4 jit_solution(9984680688154896713)
XLA Ops:
  0.6 0.8 %copy.7.ancestors = s32[5,4]{1,0:T(8,128)S(1)} copy(s32[5,4]{0,1:T(4,128)} %param.9) | data formatting | bytes 160 | tf_op args[4]
  1.4 0.0 copy-start
  1.4 1.3 %copy-done = bf16[320,2048]{1,0:T(8,128)(2,1)S(1)} copy-done((bf16[320,2048]{1,0:T(8,128)(2,1)S(1)}, bf16[320,2048]{1,0:T(8,128)(2,1)}, u32[]{:S(2)}) %copy-start) | copy-done | bytes 1310744
  2.7 0.0 copy-start.1
  2.7 1.3 %copy-done.1 = bf16[320,2048]{1,0:T(8,128)(2,1)S(1)} copy-done((bf16[320,2048]{1,0:T(8,128)(2,1)S(1)}, bf16[320,2048]{1,0:T(8,128)(2,1)}, u32[]{:S(2)}) %copy-start.1) | copy-done | bytes 1310744
  4.0 0.0 copy-start.2
  4.0 1.0 %copy-done.2 = bf16[320,512]{1,0:T(8,128)(2,1)S(1)} copy-done((bf16[320,512]{1,0:T(8,128)(2,1)S(1)}, bf16[320,512]{1,0:T(8,128)(2,1)}, u32[]{:S(2)}) %copy-start.2) | copy-done | bytes 327704
  5.0 0.0 copy-start.3
  5.0 0.7 %copy-done.3 = s32[5]{0:T(128)S(1)} copy-done((s32[5]{0:T(128)S(1)}, s32[5]{0:T(128)}, u32[]{:S(2)}) %copy-start.3) | copy-done | bytes 44
  5.7 50.0 %shard_map.68 = (bf16[320,2048]{1,0:T(8,128)(2,1)S(1)}, bf16[320,512]{1,0:T(8,128)(2,1)S(1)}) custom-call(s32[5]{0:T(128)S(1)} %copy-done.3, s32[5,4]{1,0:T(8,128)S(1)} %copy.7.ancestors, bf16[320,2048]{1,0:T(8,128)(2,1)S(1)} %copy-done, bf16[320,512]{1,0:T(8,128)(2,1)S(1)} %copy-done.2, bf16[320,2048]{1,0:T(8,128)(2,1)S(1)} %copy-done.1), custom_call_target="tpu_custom_call" | custom-call | tf_op jit(solution)/shard_map/pallas_call | solution.py:474
  55.6 1.1 %copy.10 = bf16[320,2048]{1,0:T(8,128)(2,1)} copy(bf16[320,2048]{1,0:T(8,128)(2,1)S(1)} %get-tuple-element.4) | data formatting | bytes 2621440
  56.7 0.7 %copy.11 = bf16[320,512]{1,0:T(8,128)(2,1)} copy(bf16[320,512]{1,0:T(8,128)(2,1)S(1)} %get-tuple-element.5) | data formatting | bytes 655360
Async XLA Ops:
  1.4 1.3 %copy-start = (bf16[320,2048]{1,0:T(8,128)(2,1)S(1)}, bf16[320,2048]{1,0:T(8,128)(2,1)}, u32[]{:S(2)}) copy-start(bf16[320,2048]{1,0:T(8,128)(2,1)} %query.1) | copy-start | bytes 3932164
  2.7 1.3 %copy-start.1 = (bf16[320,2048]{1,0:T(8,128)(2,1)S(1)}, bf16[320,2048]{1,0:T(8,128)(2,1)}, u32[]{:S(2)}) copy-start(bf16[320,2048]{1,0:T(8,128)(2,1)} %grad_out.1) | copy-start | bytes 3932164
  4.0 1.0 %copy-start.2 = (bf16[320,512]{1,0:T(8,128)(2,1)S(1)}, bf16[320,512]{1,0:T(8,128)(2,1)}, u32[]{:S(2)}) copy-start(bf16[320,512]{1,0:T(8,128)(2,1)} %key_value.1) | copy-start | bytes 983044
  5.0 0.7 %copy-start.3 = (s32[5]{0:T(128)S(1)}, s32[5]{0:T(128)}, u32[]{:S(2)}) copy-start(s32[5]{0:T(128)} %lengths.1) | copy-start | bytes 64

commit v2 on v1

--- a/solution.py
+++ b/solution.py
@@ -170,8 +170,9 @@
     )
 
 
-def kernel(n, kvh, group, lengths, ancestors, query, key_value, grad_out, dq_out, dkv_out, *scratch):
+def kernel(n, kvh, group, lengths_in, ancestors_in, query, key_value, grad_out, dq_out, dkv_out, *scratch):
     scratch = list(scratch)
+    lengths, ancestors, tree_in = scratch.pop(0), scratch.pop(0), scratch.pop(0)
     kv_buf = [[scratch.pop(0) for _ in range(FAR)] for _ in range(kvh)]
     last_kv, q_buf, do_buf, dq_buf, dkv_buf, lens, own, term, sent, arrived = scratch[:10]
     kv_in, last_in, q_in, do_in, dq_sem, dkv_sem, kv_send, kv_recv, len_send, len_recv, g_send, g_recv = scratch[10:]
@@ -194,6 +195,12 @@
         rows = pl.ds(j * SLOT, SLOT)
         return pltpu.make_async_copy(source.at[rows], target.at[rows], sem.at[j])
 
+    tree = [
+        pltpu.make_async_copy(lengths_in, lengths, tree_in.at[0]),
+        pltpu.make_async_copy(ancestors_in, ancestors, tree_in.at[1]),
+    ]
+    for copy in tree:
+        copy.start()
     for h in range(kvh):
         for l in range(FAR):
             kv_local(h, l).start()
@@ -208,6 +215,8 @@
         pl.semaphore_signal(
             barrier, inc=1, device_id={"leaf": lax.rem(me + k, n)}, device_id_type=pl.DeviceIdType.MESH
         )
+    for copy in tree:
+        copy.wait()
     for l in range(FAR):
         lens[me, l] = jnp.full((128,), lengths[l], jnp.int32)
     pl.semaphore_wait(barrier, n - 1)
@@ -251,10 +260,16 @@
         def _():
             kv_copy(way, s, h, l, me - 1 - s if way == 0 else me + 1 + s).wait_recv()
 
-    def own_sends(h):
-        for l in range(FAR):
-            kv_start(0, 0, h, l)
-            kv_start(1, 0, h, l)
+    def own_sends(h, sends):
+        if h == kvh:
+            return
+        for way in (0, 1):
+            before = me if way == 0 else n - 1 - me
+
+            @pl.when((before == sends) & hop_ok(way, 0))
+            def _():
+                for l in range(FAR):
+                    kv_copy(way, 0, h, l, me).start()
 
     def hop(h, s):
         for l in range(FAR):
@@ -262,6 +277,7 @@
                 kv_arrive(way, s, h, l)
                 if s + 1 < n - 1:
                     kv_start(way, s + 1, h, l)
+        own_sends(h + 1, s + 1)
 
     key_pos = lax.broadcasted_iota(jnp.int32, (SLOT, 128), 0)
     query_pos = lax.broadcasted_iota(jnp.int32, (SLOT, 128), 1) & (SLOT - 1)
@@ -273,7 +289,7 @@
         return jnp.concatenate([tile] * (lanes // 128), 1)
 
     def home(j, l):
-        return lax.div(ancestors[j, l], SEG_DEV)
+        return lax.div(ancestors[l, j], SEG_DEV)
 
     def dq_copy(h, j):
         view = (pl.ds(j * SLOT, SLOT), pl.ds(h * cols, cols))
@@ -347,22 +363,21 @@
     def g_behind(way):
         return me > 0 if way == 0 else me < n - 1
 
-    def send_terms(h, k):
-        for l in range(FAR):
-            for way in (0, 1):
-                @pl.when(g_ok(way, k))
-                def _():
-                    target = g_target(way, k)
-                    sent[h, target, l] = local_terms(h, l, target).astype(BF16)
-
-                    if k < n - 1:
-                        @pl.when(g_behind(way))
-                        def _():
-                            g_copy(way, k + 1, h, l, target).wait_recv()
-                            total = sent[h, target, l].astype(F32) + arrived[way, h, target, l].astype(F32)
-                            sent[h, target, l] = total.astype(BF16)
-
-                    g_copy(way, k, h, l, target).start()
+    def send_terms(h, k, l):
+        for way in (0, 1):
+            @pl.when(g_ok(way, k))
+            def _():
+                target = g_target(way, k)
+                sent[h, target, l] = local_terms(h, l, target).astype(BF16)
+
+                if k < n - 1:
+                    @pl.when(g_behind(way))
+                    def _():
+                        g_copy(way, k + 1, h, l, target).wait_recv()
+                        total = sent[h, target, l].astype(F32) + arrived[way, h, target, l].astype(F32)
+                        sent[h, target, l] = total.astype(BF16)
+
+                g_copy(way, k, h, l, target).start()
 
     def dkv_copy(h, j):
         view = (pl.ds(j * SLOT, SLOT), pl.ds(h * width, width))
@@ -372,16 +387,15 @@
         dkv_buf[pl.ds(FAR * SLOT, SLOT), pl.ds(h * width, width)] = own[h, FAR].astype(BF16)
         dkv_copy(h, FAR).start()
 
-    def finish(h):
-        for l in range(FAR):
-            own[h, l] = own[h, l] + local_terms(h, l, me).astype(BF16).astype(F32)
-            for way in (0, 1):
-                @pl.when(g_behind(way))
-                def _():
-                    g_copy(way, 1, h, l, me).wait_recv()
-                    own[h, l] = own[h, l] + arrived[way, h, me, l].astype(F32)
-            dkv_buf[pl.ds(l * SLOT, SLOT), pl.ds(h * width, width)] = own[h, l].astype(BF16)
-            dkv_copy(h, l).start()
+    def finish(h, l):
+        own[h, l] = own[h, l] + local_terms(h, l, me).astype(BF16).astype(F32)
+        for way in (0, 1):
+            @pl.when(g_behind(way))
+            def _():
+                g_copy(way, 1, h, l, me).wait_recv()
+                own[h, l] = own[h, l] + arrived[way, h, me, l].astype(F32)
+        dkv_buf[pl.ds(l * SLOT, SLOT), pl.ds(h * width, width)] = own[h, l].astype(BF16)
+        dkv_copy(h, l).start()
 
     for k in range(1, n):
         lens_copy(k).start()
@@ -392,6 +406,7 @@
     for h in range(1, kvh):
         for l in range(FAR):
             kv_local(h, l).wait()
+    own_sends(1, 0)
     for h in range(kvh):
         last_local(h).wait()
     for k in range(1, n):
@@ -404,26 +419,30 @@
         compute(h, 0)
     for s in range(n - 1):
         hop(0, s)
-    for h in range(kvh):
-        steps = []
-        if h + 1 < kvh:
-            own_sends(h + 1)
-            steps += [functools.partial(hop, h + 1, s) for s in range(n - 1)]
-        if h > 0:
-            steps += [functools.partial(send_terms, h - 1, k) for k in range(n - 1, 0, -1)]
-        for j in range(1, SEG_DEV):
-            if steps and h > 0:
-                steps.pop(0)()
+
+    order = [(h, j) for h in range(kvh) for j in range(FAR, 0, -1)]
+    for step in range(len(order) + n):
+        if step < len(order):
+            h, j = order[step]
             compute(h, j)
-            if steps and h == 0:
-                steps.pop(0)()
-        for step in steps:
-            step()
-        finish_last(h)
-    for k in range(n - 1, 0, -1):
-        send_terms(kvh - 1, k)
-    for h in range(kvh):
-        finish(h)
+            if h + 1 < kvh and FAR - j < n - 2:
+                hop(h + 1, FAR - j)
+        for k in range(n - 1, 0, -1):
+            behind = step - (n - 1 - k)
+            if 0 <= behind < len(order):
+                done_h, done_j = order[behind]
+                send_terms(done_h, k, done_j - 1)
+        behind = step - n
+        if 0 <= behind < len(order):
+            done_h, done_j = order[behind]
+            finish(done_h, done_j - 1)
+        if step < len(order):
+            h, j = order[step]
+            if j == 1:
+                finish_last(h)
+                for s in range(n - 2 if FAR > n - 2 else FAR, n - 1):
+                    if h + 1 < kvh:
+                        hop(h + 1, s)
 
     for k in range(1, n):
         for way in (0, 1):
@@ -451,7 +470,13 @@
     kvh = key_value.shape[1] // width
     group = query.shape[1] // (kvh * HD)
     tile = (SLOT, width)
-    scratch = [pltpu.VMEM((n,) + tile, BF16) for _ in range(kvh * FAR)]
+    dma = pltpu.SemaphoreType.DMA
+    scratch = [
+        pltpu.SMEM(lengths.shape, jnp.int32),
+        pltpu.SMEM(ancestors.shape[::-1], jnp.int32),
+        dma((2,)),
+    ]
+    scratch += [pltpu.VMEM((n,) + tile, BF16) for _ in range(kvh * FAR)]
     scratch += [
         pltpu.VMEM((kvh,) + tile, BF16),
         pltpu.VMEM(query.shape, BF16),
@@ -464,12 +489,10 @@
         pltpu.VMEM((kvh, n, FAR) + tile, BF16),
         pltpu.VMEM((2, kvh, n, FAR) + tile, BF16),
     ]
-    dma = pltpu.SemaphoreType.DMA
     scratch += [dma((kvh, FAR)), dma((kvh,)), dma((SEG_DEV,)), dma((SEG_DEV,))]
     scratch += [dma((kvh, SEG_DEV)), dma((kvh, SEG_DEV))]
     scratch += [dma((2, n - 1, kvh, FAR)), dma((2, n - 1, kvh, FAR)), dma((n - 1,)), dma((n - 1,))]
     scratch += [dma((2, n - 1, kvh, FAR)), dma((2, n - 1, kvh, FAR))]
-    smem = pl.BlockSpec(memory_space=pltpu.SMEM)
     anywhere = pl.BlockSpec(memory_space=pl.ANY)
     return pl.pallas_call(
         functools.partial(kernel, n, kvh, group),
@@ -477,13 +500,13 @@
             jax.ShapeDtypeStruct(query.shape, BF16),
             jax.ShapeDtypeStruct(key_value.shape, BF16),
         ),
-        in_specs=[smem, smem, anywhere, anywhere, anywhere],
+        in_specs=[anywhere] * 5,
         out_specs=(anywhere, anywhere),
         scratch_shapes=scratch,
         compiler_params=pltpu.CompilerParams(
-            collective_id=0, has_side_effects=True, vmem_limit_bytes=48 * 1024 * 1024
+            collective_id=0, has_side_effects=True, vmem_limit_bytes=60 * 1024 * 1024
         ),
-    )(lengths, ancestors, query, key_value, grad_out)
+    )(lengths, ancestors.T, query, key_value, grad_out)
 
 
 def on_device(query, key_value, grad_out, lengths, ancestors):

time: 57.7 us -> 50.5 us (0.88)
  Pallas kernels: 50 us -> 46.4 us
  local copies, waits for them, and re-layouts: 6.81 us -> 3.29 us
    pallas_call x1, Pallas kernels: 50 us -> 46.4 us  [line_device(): pl.pallas_call(functools.partial(kernel, n, kvh, group), out_shape=(jax.S...]
    unnamed x11 -> x4, local copies, waits for them, and re-layouts: 6.81 us -> 3.29 us
where the time goes in v2:
time: 50.5 us; the launch traced here: 50.4 us
  Pallas kernels  46.4 us (92%)
  local copies, waits for them, and re-layouts  3.29 us (7%)
  between operations  0.65 us (1%)
    pallas_call x1, Pallas kernels, line_device(): pl.pallas_call(functools.partial(kernel, n, kvh, group), out_shape=(jax.S...  46.4 us
    unnamed x4, local copies, waits for them, and re-layouts  3.29 us

profile of v2, /device:TPU:0, one launch (start us, length us, event | category | flops | bytes accessed | tf_op | source)
XLA Modules:
  0.0 50.4 jit_solution(10869106269451171910)
XLA Ops:
  0.6 46.4 %shard_map.68 = (bf16[320,2048]{1,0:T(8,128)(2,1)}, bf16[320,512]{1,0:T(8,128)(2,1)}) custom-call(s32[5]{0:T(128)} %lengths_in.1, s32[4,5]{1,0:T(4,128)} %bitcast.1, bf16[320,2048]{1,0:T(8,128)(2,1)} %query.1, bf16[320,512]{1,0:T(8,128)(2,1)} %key_value.1, bf16[320,2048]{1,0:T(8,128)(2,1)} %grad_out.1), custom_call_target="tpu_custom_call" | custom-call | tf_op jit(solution)/shard_map/pallas_call | solution.py:497
  47.1 0.0 copy-start
  47.1 2.6 %copy.9 = bf16[320,2048]{1,0:T(8,128)(2,1)} copy(bf16[320,2048]{1,0:T(8,128)(2,1)} %get-tuple-element.4) | data formatting | bytes 2621440
  49.6 0.0 copy-done
  49.6 0.7 %copy.10 = bf16[320,512]{1,0:T(8,128)(2,1)} copy(bf16[320,512]{1,0:T(8,128)(2,1)S(1)} %copy-done) | data formatting | bytes 655360
Async XLA Ops:
  47.1 2.6 %copy-start = (bf16[320,512]{1,0:T(8,128)(2,1)S(1)}, bf16[320,512]{1,0:T(8,128)(2,1)}, u32[]{:S(2)}) copy-start(bf16[320,512]{1,0:T(8,128)(2,1)} %get-tuple-element.5) | copy-start | bytes 983044

commit v3 on v2

--- a/solution.py
+++ b/solution.py
@@ -363,20 +363,24 @@
     def g_behind(way):
         return me > 0 if way == 0 else me < n - 1
 
-    def send_terms(h, k, l):
+    def lead_terms(h, l):
         for way in (0, 1):
-            @pl.when(g_ok(way, k))
+            @pl.when(me == (0 if way == 0 else n - 1))
+            def _():
+                for k in range(n - 1, 0, -1):
+                    target = g_target(way, k)
+                    sent[h, target, l] = local_terms(h, l, target).astype(BF16)
+                    g_copy(way, k, h, l, target).start()
+
+    def relay_terms(h, k, l):
+        for way in (0, 1):
+            @pl.when(g_ok(way, k) & g_behind(way))
             def _():
                 target = g_target(way, k)
-                sent[h, target, l] = local_terms(h, l, target).astype(BF16)
-
-                if k < n - 1:
-                    @pl.when(g_behind(way))
-                    def _():
-                        g_copy(way, k + 1, h, l, target).wait_recv()
-                        total = sent[h, target, l].astype(F32) + arrived[way, h, target, l].astype(F32)
-                        sent[h, target, l] = total.astype(BF16)
-
+                g_copy(way, k + 1, h, l, target).wait_recv()
+                total = local_terms(h, l, target).astype(BF16).astype(F32)
+                total = total + arrived[way, h, target, l].astype(F32)
+                sent[h, target, l] = total.astype(BF16)
                 g_copy(way, k, h, l, target).start()
 
     def dkv_copy(h, j):
@@ -425,13 +429,14 @@
         if step < len(order):
             h, j = order[step]
             compute(h, j)
+            lead_terms(h, j - 1)
             if h + 1 < kvh and FAR - j < n - 2:
                 hop(h + 1, FAR - j)
-        for k in range(n - 1, 0, -1):
+        for k in range(n - 2, 0, -1):
             behind = step - (n - 1 - k)
             if 0 <= behind < len(order):
                 done_h, done_j = order[behind]
-                send_terms(done_h, k, done_j - 1)
+                relay_terms(done_h, k, done_j - 1)
         behind = step - n
         if 0 <= behind < len(order):
             done_h, done_j = order[behind]

time: 50.5 us -> 50.1 us (level)
  no operation moved by 1% of the time
where the time goes in v3:
time: 50.1 us; the launch traced here: 50 us
  Pallas kernels  46 us (92%)
  local copies, waits for them, and re-layouts  3.29 us (7%)
  between operations  0.65 us (1%)
    pallas_call x1, Pallas kernels, line_device(): pl.pallas_call(functools.partial(kernel, n, kvh, group), out_shape=(jax.S...  46 us
    unnamed x4, local copies, waits for them, and re-layouts  3.29 us

profile of v3, /device:TPU:0, one launch (start us, length us, event | category | flops | bytes accessed | tf_op | source)
XLA Modules:
  0.0 50.0 jit_solution(2664739843680343470)
XLA Ops:
  0.6 46.0 %shard_map.68 = (bf16[320,2048]{1,0:T(8,128)(2,1)}, bf16[320,512]{1,0:T(8,128)(2,1)}) custom-call(s32[5]{0:T(128)} %lengths_in.1, s32[4,5]{1,0:T(4,128)} %bitcast.1, bf16[320,2048]{1,0:T(8,128)(2,1)} %query.1, bf16[320,512]{1,0:T(8,128)(2,1)} %key_value.1, bf16[320,2048]{1,0:T(8,128)(2,1)} %grad_out.1), custom_call_target="tpu_custom_call" | custom-call | tf_op jit(solution)/shard_map/pallas_call | solution.py:502
  46.6 0.0 copy-start
  46.7 2.6 %copy.9 = bf16[320,2048]{1,0:T(8,128)(2,1)} copy(bf16[320,2048]{1,0:T(8,128)(2,1)} %get-tuple-element.4) | data formatting | bytes 2621440
  49.2 0.0 copy-done
  49.2 0.7 %copy.10 = bf16[320,512]{1,0:T(8,128)(2,1)} copy(bf16[320,512]{1,0:T(8,128)(2,1)S(1)} %copy-done) | data formatting | bytes 655360
Async XLA Ops:
  46.6 2.6 %copy-start = (bf16[320,512]{1,0:T(8,128)(2,1)S(1)}, bf16[320,512]{1,0:T(8,128)(2,1)}, u32[]{:S(2)}) copy-start(bf16[320,512]{1,0:T(8,128)(2,1)} %get-tuple-element.5) | copy-start | bytes 983044
